TPU v7x, 32 devices: a whole 2x2x4 slice. The times are simulated.
32 devices in a mesh: rep: 4 (over x, core), ep: 8 (over z, y).
Axes of the slice: x: 2, y: 2, z: 4, core: 2. Of those that a mesh axis runs over, the one named last changes fastest.
Arguments:
- tokens: bfloat16 [4096, 2048], P(('rep', 'ep')), may hold values from -6 to 6
- expert_ids: int32 [4096, 8], P(('rep', 'ep')), may hold values from 0 to 31, as said below
- route_weight: float32 [4096, 8], P(('rep', 'ep')), may hold values from 0.05 to 1
- hot_plan: int32 [8], replicated, may hold values from 0 to 3, as said below
- gate_proj: bfloat16 [32, 2048, 768], P(('rep', 'ep')), may hold values from -0.125 to 0.125
- up_proj: bfloat16 [32, 2048, 768], P(('rep', 'ep')), may hold values from -0.125 to 0.125
- down_proj: bfloat16 [32, 768, 2048], P(('rep', 'ep')), may hold values from -0.21875 to 0.21875
Outputs:
- layer_out: bfloat16 [4096, 2048], P(('rep', 'ep'))
- served_load: float32 [32], replicated
Inputs may be any that keep to these rules, and one draw needn't show every extreme that they name: `expert_ids`: within the rows of one device (aligned blocks of 128 tokens) a hot expert is named at most 64 times and any other expert at most 24 times. Some expert that is not hot is named exactly 24 times in every block, and the hot expert of some column exactly 64 times in every block. Expert hot_plan[c] * 8 + c is the hot expert of column c.
All inputs are finite; a program needn't handle non-finite values.
Results may differ from a plain program's by a relative error of at most 0.0057.
Values may be sent and summed in bfloat16 or wider, within the bound.
A program may use at most 128 MiB of HBM per device.

v0:
```python
import jax
import jax.numpy as jnp
from jax import lax
from jax.sharding import PartitionSpec as P


def from_root(array, axis, root):
    mine = lax.axis_index(axis) == root
    return lax.psum(jnp.where(mine, array, jnp.zeros_like(array)), axis)


def expert_ffn(slot_rows, gate_mat, up_mat, down_mat):
    layout = slot_rows.shape
    flattened = slot_rows.reshape(-1, layout[-1])
    gate_in = jnp.dot(flattened, gate_mat, preferred_element_type=jnp.float32)
    up_in = jnp.dot(flattened, up_mat, preferred_element_type=jnp.float32)
    hidden = (jax.nn.silu(gate_in) * up_in).astype(jnp.bfloat16)
    result = jnp.dot(hidden, down_mat, preferred_element_type=jnp.float32).astype(jnp.bfloat16)
    return result.reshape(layout)


def local(tokens, expert_ids, route_weight, hot_plan, gate_proj, up_proj, down_proj):
    n_rep = lax.axis_size("rep")
    n_ep = lax.axis_size("ep")
    devices = n_rep * n_ep
    my_row = lax.axis_index("rep")
    my_col = lax.axis_index("ep")
    tok_rows, top_count = expert_ids.shape
    model_width = tokens.shape[1]
    routed = tok_rows * top_count
    cool_cap = max(2, 3 * routed // (4 * devices))
    hot_cap = max(4, 2 * routed // devices)
    flat_ids = expert_ids.reshape(-1)
    expert_range = jnp.arange(devices, dtype=jnp.int32)
    column_range = jnp.arange(n_ep, dtype=jnp.int32)
    one_hot = (flat_ids[:, None] == expert_range[None, :]).astype(jnp.int32)
    own_counts = jnp.sum(one_hot, axis=0, dtype=jnp.int32)
    row_match = (jnp.arange(n_rep, dtype=jnp.int32) == my_row)[:, None]
    placed = jnp.where(row_match, own_counts[None, :], jnp.zeros_like(own_counts)[None, :])
    row_counts = lax.psum(placed, ("rep", "ep"))
    same_column = expert_range[:, None] % n_ep == column_range[None, :]
    same_row = expert_range[:, None] // n_ep == hot_plan[None, :]
    hot_flag = jnp.any(same_column & same_row, axis=1)
    counts = jnp.sum(row_counts, axis=0, dtype=jnp.int32)
    hot_expert = hot_plan * n_ep + column_range
    copy_rows = row_counts[:, hot_expert].reshape(-1)
    served = jnp.where(hot_flag, jnp.zeros_like(counts), counts) + copy_rows
    served_load = served.astype(jnp.float32) / jnp.float32(routed)
    is_hot = jnp.sum(one_hot * hot_flag.astype(jnp.int32)[None, :], axis=1, dtype=jnp.int32) > 0
    ordinal = jnp.sum((jnp.cumsum(one_hot, axis=0) - 1) * one_hot, axis=1)
    home_col = flat_ids % n_ep
    source = jnp.arange(routed, dtype=jnp.int32) // top_count

    def pack_rows(slot, total):
        owners = jnp.zeros((total + 1,), jnp.int32).at[slot].set(source)[:total]
        filled = jnp.zeros((total + 1,), jnp.bool_).at[slot].set(True)[:total]
        return jnp.where(filled[:, None], tokens[owners], jnp.zeros((), jnp.bfloat16))

    home_total = devices * cool_cap
    home_slot = jnp.where(is_hot, home_total, flat_ids * cool_cap + ordinal)
    copy_total = n_ep * hot_cap
    copy_slot = jnp.where(is_hot, home_col * hot_cap + ordinal, copy_total)
    copy_send = pack_rows(copy_slot, copy_total).reshape(n_ep, hot_cap, model_width)
    copied = (
        from_root(gate_proj[0], "rep", hot_plan[my_col]),
        from_root(up_proj[0], "rep", hot_plan[my_col]),
        from_root(down_proj[0], "rep", hot_plan[my_col]),
    )
    copy_done = expert_ffn(
        lax.all_to_all(copy_send, "ep", split_axis=0, concat_axis=0, tiled=True),
        copied[0],
        copied[1],
        copied[2],
    )
    copy_back = lax.all_to_all(copy_done, "ep", split_axis=0, concat_axis=0, tiled=True)
    copy_result = copy_back.reshape(copy_total, model_width)[jnp.minimum(copy_slot, copy_total - 1)]
    home_send = pack_rows(home_slot, home_total).reshape(devices, cool_cap, model_width)
    home_done = expert_ffn(
        lax.all_to_all(home_send, ("rep", "ep"), split_axis=0, concat_axis=0, tiled=True),
        gate_proj[0],
        up_proj[0],
        down_proj[0],
    )
    home_back = lax.all_to_all(home_done, ("rep", "ep"), split_axis=0, concat_axis=0, tiled=True)
    home_result = home_back.reshape(home_total, model_width)[jnp.minimum(home_slot, home_total - 1)]
    gathered = jnp.where(is_hot[:, None], copy_result, home_result)
    shares = route_weight / jnp.sum(route_weight, axis=1, keepdims=True)
    combined = jnp.sum(
        shares[:, :, None] * gathered.reshape(tok_rows, top_count, model_width).astype(jnp.float32),
        axis=1,
    )
    return (combined.astype(jnp.bfloat16), served_load)


def solution(mesh):
    placed = (
        P(("rep", "ep"), None),
        P(("rep", "ep"), None),
        P(("rep", "ep"), None),
        P(),
        P(("rep", "ep"), None, None),
        P(("rep", "ep"), None, None),
        P(("rep", "ep"), None, None),
    )
    return jax.shard_map(
        local, mesh=mesh, in_specs=placed, out_specs=(P(("rep", "ep"), None), P()), check_vma=False
    )
```

profile of v0, /device:TPU:8, one launch (start us, length us, event | category | flops | bytes accessed | tf_op | source)
XLA Modules:
  0.0 446.3 jit_solution(6926824675392805073)
XLA Ops:
  8.3 9.0 %reduce-window.6 = s32[32,8,128]{2,1,0:T(8,128)S(1)} reduce-window(s32[32,8,128]{2,1,0:T(8,128)S(1)} %fusion.11, s32[]{:T(128)} %constant.55.clone.1), window={size=1x1x128 pad=0_0x0_0x127_0}, to_apply=%region_3.4 | reduce-window | flops 4161536 | bytes 262148 | tf_op jit(solution)/shard_map/reduce-window
  18.8 4.3 scatter_custom_fusion.1
  23.1 4.3 scatter_custom_fusion
  31.6 6.4 %all-to-all-start = ((bf16[8,64,2048]{2,1,0:T(8,128)(2,1)}), bf16[8,64,2048]{2,1,0:T(8,128)(2,1)S(1)}, u32[]{:S(2)}, u32[]{:S(2)}) async-start(bf16[8,64,2048]{2,1,0:T(8,128)(2,1)} %broadcast_select_fusion.1), calls=%async_computation | async-start | bytes 4194304 | tf_op jit(solution)/shard_map/all_to_all | solution.py:70
  39.3 3.9 bitcast_select_fusion.1
  44.2 3.0 bitcast_select_fusion.2
  47.3 4.5 %scatter_custom_fusion.3 = s32[769]{0:T(1024)S(1)} fusion(s32[1024]{0:T(1024)S(1)} %bitcast.74, s32[1024]{0:T(1024)S(1)} %add_select_fusion, s32[]{:T(128)} %constant.55.clone.1), kind=kCustom, calls=%fused_computation.65 | custom fusion | bytes 3080 | tf_op jit(solution)/shard_map/scatter | solution.py:55
  51.8 4.3 scatter_custom_fusion.2
  56.1 4.3 gather_fusion.2
  60.5 3.8 broadcast_select_fusion
  64.3 19.5 %all-to-all-done = bf16[8,64,2048]{2,1,0:T(8,128)(2,1)S(1)} async-done(((bf16[8,64,2048]{2,1,0:T(8,128)(2,1)}), bf16[8,64,2048]{2,1,0:T(8,128)(2,1)S(1)}, u32[]{:S(2)}, u32[]{:S(2)}) %all-to-all-start) | async-done | bytes 2097184 | tf_op jit(solution)/shard_map/all_to_all | solution.py:70
  83.8 5.9 %all-to-all-start.2 = ((bf16[32,24,2048]{2,1,0:T(8,128)(2,1)}), bf16[32,24,2048]{2,1,0:T(8,128)(2,1)}, u32[]{:S(2)}, u32[]{:S(2)}) async-start(bf16[32,24,2048]{2,1,0:T(8,128)(2,1)} %broadcast_select_fusion), calls=%async_computation.2 | async-start | bytes 6291456 | tf_op jit(solution)/shard_map/all_to_all | solution.py:79
  89.7 163.3 %all-reduce.3.cloned.1.call-done = (bf16[768,2048]{1,0:T(8,128)(2,1)}, bf16[2048,768]{1,0:T(8,128)(2,1)}, bf16[2048,768]{1,0:T(8,128)(2,1)}) async-done(((bf16[768,2048]{1,0:T(8,128)(2,1)}, bf16[2048,768]{1,0:T(8,128)(2,1)}, bf16[2048,768]{1,0:T(8,128)(2,1)}), (bf16[768,2048]{1,0:T(8,128)(2,1)}, bf16[2048,768]{1,0:T(8,128)(2,1)}, bf16[2048,768]{1,0:T(8,128)(2,1)})) %all-reduce.3.cloned.1.call-update) | async-done | bytes 9437200 | tf_op jit(solution)/shard_map/psum | solution.py:9
  253.0 4.8 %fusion.30 = f32[512,768]{1,0:T(8,128)} fusion(bf16[512,2048]{1,0:T(8,128)(2,1)S(1)} %bitcast.63, bf16[2048,768]{1,0:T(8,128)(2,1)} %get-tuple-element.6), kind=kOutput, calls=%fused_computation.84 | convolution fusion | flops 1610612736 | bytes 6815744 | tf_op jit(solution)/shard_map/dot_general | solution.py:15
  257.8 8.6 %convolution_convert_fusion.1 = bf16[512,2048]{1,0:T(8,128)(2,1)} fusion(bf16[768,2048]{1,0:T(8,128)(2,1)} %get-tuple-element.5, f32[512,768]{1,0:T(8,128)} %fusion.30, bf16[512,2048]{1,0:T(8,128)(2,1)S(1)} %bitcast.64, bf16[2048,768]{1,0:T(8,128)(2,1)} %get-tuple-element.7), kind=kOutput, calls=%fused_computation.21 | convolution fusion | flops 3224633344 | bytes 12058624 | tf_op jit(solution)/shard_map/dot_general | solution.py:18
  266.5 6.1 %all-to-all-start.1 = ((bf16[8,64,2048]{2,1,0:T(8,128)(2,1)}), bf16[8,64,2048]{2,1,0:T(8,128)(2,1)S(1)}, u32[]{:S(2)}, u32[]{:S(2)}) async-start(bf16[8,64,2048]{2,1,0:T(8,128)(2,1)} %bitcast.65), calls=%async_computation.1 | async-start | bytes 4194304 | tf_op jit(solution)/shard_map/all_to_all | solution.py:75
  272.5 6.9 %fusion.1 = f32[768,768]{1,0:T(8,128)} fusion(bf16[768,2048]{1,0:T(8,128)(2,1)} %bitcast.16, bf16[1,2048,768]{2,1,0:T(8,128)(2,1)} %param.12), kind=kOutput, calls=%fused_computation.14 | convolution fusion | flops 2415919104 | bytes 8650752 | tf_op jit(solution)/shard_map/dot_general | solution.py:16
  279.4 11.9 %convolution_convert_fusion = bf16[768,2048]{1,0:T(8,128)(2,1)} fusion(bf16[1,768,2048]{2,1,0:T(8,128)(2,1)} %param.13, f32[768,768]{1,0:T(8,128)} %fusion.1, bf16[768,2048]{1,0:T(8,128)(2,1)} %bitcast.16, bf16[1,2048,768]{2,1,0:T(8,128)(2,1)} %param.11), kind=kOutput, calls=%fused_computation.11 | convolution fusion | flops 4836950016 | bytes 14942208 | tf_op jit(solution)/shard_map/dot_general | solution.py:18
  291.3 26.8 %all-to-all-done.1 = bf16[8,64,2048]{2,1,0:T(8,128)(2,1)S(1)} async-done(((bf16[8,64,2048]{2,1,0:T(8,128)(2,1)}), bf16[8,64,2048]{2,1,0:T(8,128)(2,1)S(1)}, u32[]{:S(2)}, u32[]{:S(2)}) %all-to-all-start.1) | async-done | bytes 2097184 | tf_op jit(solution)/shard_map/all_to_all | solution.py:75
  318.1 5.7 %all-to-all-start.3 = ((bf16[32,24,2048]{2,1,0:T(8,128)(2,1)}), bf16[32,24,2048]{2,1,0:T(8,128)(2,1)}, u32[]{:S(2)}, u32[]{:S(2)}) async-start(bf16[32,24,2048]{2,1,0:T(8,128)(2,1)} %bitcast.62), calls=%async_computation.3 | async-start | bytes 6291456 | tf_op jit(solution)/shard_map/all_to_all | solution.py:84
  324.2 89.7 %psum.31 = s32[4,32]{0,1:T(8,128)S(1)} all-reduce(s32[4,32]{0,1:T(8,128)S(1)} %broadcast_select_fusion.2), channel_id=1, replica_groups=mesh['rep'=4,'ep'=8] {'rep','ep'}, use_global_device_ids=true, to_apply=%region_15.16 | all-reduce | flops 128 | bytes 1024 | tf_op jit(solution)/shard_map/psum | solution.py:40
  415.3 6.0 %gather_fusion.1 = bf16[1024,2048]{1,0:T(8,128)(2,1)} fusion(bf16[512,2048]{1,0:T(8,128)(2,1)S(1)} %bitcast.59, s32[1024]{0:T(1024)S(1)} %broadcast_clamp_fusion.1), kind=kCustom, calls=%fused_computation.1 | custom fusion | bytes 8392704 | tf_op jit(solution)/shard_map/gather | solution.py:76
  421.3 11.2 %gather_fusion.3 = bf16[1024,2048]{1,0:T(8,128)(2,1)} fusion(bf16[768,2048]{1,0:T(8,128)(2,1)} %bitcast.18, s32[1024]{0:T(1024)S(1)} %broadcast_clamp_fusion), kind=kCustom, calls=%fused_computation.3 | custom fusion | bytes 8392704 | tf_op jit(solution)/shard_map/gather | solution.py:85
  432.5 7.0 %multiply_reduce_fusion = bf16[128,2048]{1,0:T(8,128)(2,1)} fusion(bf16[1024,2048]{1,0:T(8,128)(2,1)} %gather_fusion.3, bf16[1024,2048]{1,0:T(8,128)(2,1)} %gather_fusion.1, f32[128,8]{1,0:T(8,128)S(1)} %copy.18, pred[128,8]{1,0:T(8,128)(4,1)S(1)} %gt.32), kind=kLoop, calls=%fused_computation.9 | loop fusion | flops 8126464 | bytes 8918016 | tf_op jit(solution)/shard_map/reduce_sum | solution.py:88
  (62 shorter events, 10.1 us)
Async XLA Ops:
  7.2 20.4 %copy-start = (bf16[128,2048]{1,0:T(8,128)(2,1)S(1)}, bf16[128,2048]{1,0:T(8,128)(2,1)}, u32[]{:S(2)}) copy-start(bf16[128,2048]{1,0:T(8,128)(2,1)} %param.7) | copy-start | bytes 1572868
  31.6 6.4 %copy-start.5 = (s32[8]{0:T(128)S(1)}, s32[8]{0:T(128)}, u32[]{:S(2)}) copy-start(s32[8]{0:T(128)} %param.10) | copy-start | bytes 100
  31.6 52.2 %all-to-all-start = ((bf16[8,64,2048]{2,1,0:T(8,128)(2,1)}), bf16[8,64,2048]{2,1,0:T(8,128)(2,1)S(1)}, u32[]{:S(2)}, u32[]{:S(2)}) async-start(bf16[8,64,2048]{2,1,0:T(8,128)(2,1)} %broadcast_select_fusion.1), calls=%async_computation | async-start | bytes 4194304 | tf_op jit(solution)/shard_map/all_to_all | solution.py:70
  38.0 215.0 %all-reduce.3.cloned.1.call-start = ((), (), s32[]{:S(2)}) async-start(), calls=%async_computation.4 | async-start | bytes 18874368 | tf_op jit(solution)/shard_map/psum | solution.py:9
  39.3 3.9 copy-start.2
  39.3 4.9 %copy-start.3 = (bf16[1,2048,768]{2,1,0:T(8,128)(2,1)S(1)}, bf16[1,2048,768]{2,1,0:T(8,128)(2,1)}, u32[]{:S(2)}) copy-start(bf16[1,2048,768]{2,1,0:T(8,128)(2,1)} %param.11) | copy-start | bytes 9437188
  83.8 182.6 %all-to-all-start.2 = ((bf16[32,24,2048]{2,1,0:T(8,128)(2,1)}), bf16[32,24,2048]{2,1,0:T(8,128)(2,1)}, u32[]{:S(2)}, u32[]{:S(2)}) async-start(bf16[32,24,2048]{2,1,0:T(8,128)(2,1)} %broadcast_select_fusion), calls=%async_computation.2 | async-start | bytes 6291456 | tf_op jit(solution)/shard_map/all_to_all | solution.py:79
  266.5 51.7 %all-to-all-start.1 = ((bf16[8,64,2048]{2,1,0:T(8,128)(2,1)}), bf16[8,64,2048]{2,1,0:T(8,128)(2,1)S(1)}, u32[]{:S(2)}, u32[]{:S(2)}) async-start(bf16[8,64,2048]{2,1,0:T(8,128)(2,1)} %bitcast.65), calls=%async_computation.1 | async-start | bytes 4194304 | tf_op jit(solution)/shard_map/all_to_all | solution.py:75
  318.1 5.9 %copy-start.4 = (f32[128,8]{0,1:T(8,128)S(1)}, f32[128,8]{0,1:T(8,128)}, u32[]{:S(2)}) copy-start(f32[128,8]{0,1:T(8,128)} %param.9) | copy-start | bytes 12292
  318.1 103.2 %all-to-all-start.3 = ((bf16[32,24,2048]{2,1,0:T(8,128)(2,1)}), bf16[32,24,2048]{2,1,0:T(8,128)(2,1)}, u32[]{:S(2)}, u32[]{:S(2)}) async-start(bf16[32,24,2048]{2,1,0:T(8,128)(2,1)} %bitcast.62), calls=%async_computation.3 | async-start | bytes 6291456 | tf_op jit(solution)/shard_map/all_to_all | solution.py:84
  421.3 18.2 %copy-start.1 = (bf16[128,2048]{1,0:T(8,128)(2,1)S(1)}, bf16[128,2048]{1,0:T(8,128)(2,1)}, u32[]{:S(2)}) copy-start(bf16[128,2048]{1,0:T(8,128)(2,1)} %param.7) | copy-start | bytes 1572868
Sparse Core Ops, SparseCore 0:
  47.4 205.5 all-reduce.2
where the time goes:
time: 450 us; the launch traced here: 446 us
  waiting for transfers between devices  210 us (47%)
  blocking collectives  89.7 us (20%)
  local copies, waits for them, and re-layouts  45.5 us (10%)
  matrix products  32.3 us (7%)
  other arithmetic  30.2 us (7%)
  starting transfers between devices  24.1 us (5%)
  between operations  14.9 us (3%)
    psum x1, waiting for transfers between devices, from_root(): return lax.psum(jnp.where(mine, array, jnp.zeros_like(array)), axis)  163 us
    psum x1, blocking collectives, local(): row_counts = lax.psum(placed, ('rep', 'ep'))  89.7 us
    all_to_all x1, waiting for transfers between devices, local(): lax.all_to_all(copy_done, 'ep', split_axis=0, concat_axis=0, tiled=True)  26.8 us
    dot_general x2, matrix products, expert_ffn(): jnp.dot(hidden, down_mat, preferred_element_type=jnp.float32)  20.5 us
    all_to_all x1, waiting for transfers between devices, local(): lax.all_to_all(copy_send, 'ep', split_axis=0, concat_axis=0, tiled=True)  19.5 us
    gather x1, local copies, waits for them, and re-layouts, local(): home_back.reshape(home_total, model_width)  11.2 us
    another operation x2, other arithmetic  9.04 us
  transfers between devices with their start and end apart: 5, of which 3 were waited for; matrix products, arithmetic and copies ran while one was open for 14% of the time, Pallas kernels for 0%

commit v1 on v0

v1 whole, which is shorter than its diff:
```python
import functools

import jax
import jax.numpy as jnp
from jax import lax
from jax.experimental import pallas as pl
from jax.experimental.pallas import tpu as pltpu
from jax.sharding import PartitionSpec as P

AXES = ("rep", "ep")


def expert_kernel(cap, ids_ref, share_ref, x_ref, gate_ref, up_ref, down_ref, out_ref, sel, res):
    blocks, top, rows = ids_ref.shape
    me = (lax.axis_index("rep") * lax.axis_size("ep") + lax.axis_index("ep")).astype(jnp.float32)
    earlier = lax.broadcasted_iota(jnp.int32, (rows, rows), 0) < lax.broadcasted_iota(
        jnp.int32, (rows, rows), 1
    )
    earlier = earlier.astype(jnp.bfloat16)
    slots = lax.broadcasted_iota(jnp.int32, (cap, rows), 0).astype(jnp.float32)
    picks = []
    scales = []
    for b in range(blocks):
        match = ids_ref[b] == me
        weight = jnp.sum(jnp.where(match, share_ref[b], 0.0), axis=0, keepdims=True)
        named = jnp.max(match.astype(jnp.float32), axis=0, keepdims=True)
        before = jnp.dot(
            jnp.broadcast_to(named, (8, rows)).astype(jnp.bfloat16),
            earlier,
            preferred_element_type=jnp.float32,
        )[0:1]
        hit = (slots == before) & (named > 0.0)
        pick = jnp.where(hit, 1.0, 0.0)
        picks.append(pick.astype(jnp.bfloat16))
        scales.append(jnp.sum(pick * weight, axis=1, keepdims=True))
        sel[b * cap : (b + 1) * cap, :] = jnp.dot(
            picks[b], x_ref[b], preferred_element_type=jnp.float32
        ).astype(jnp.bfloat16)
    gate_in = jnp.dot(sel[...], gate_ref[...], preferred_element_type=jnp.float32)
    up_in = jnp.dot(sel[...], up_ref[...], preferred_element_type=jnp.float32)
    hidden = (gate_in / (1.0 + jnp.exp(-gate_in)) * up_in).astype(jnp.bfloat16)
    done = jnp.dot(hidden, down_ref[...], preferred_element_type=jnp.float32)
    for b in range(blocks):
        part = slice(b * cap, (b + 1) * cap)
        res[part, :] = (done[part] * scales[b]).astype(jnp.bfloat16)
    for b in range(blocks):
        out_ref[b] = lax.dot_general(
            picks[b],
            res[b * cap : (b + 1) * cap, :],
            (((0,), (0,)), ((), ())),
            preferred_element_type=jnp.float32,
        ).astype(jnp.bfloat16)


def run_expert(x, ids, shares, gate, up, down, cap):
    blocks, rows, width = x.shape
    top = ids.shape[1]
    hidden = gate.shape[1]
    group = 8 if blocks % 8 == 0 else 1
    whole = lambda shape: pl.BlockSpec(shape, lambda i: (0, 0), pipeline_mode=pl.Buffered(1))
    return pl.pallas_call(
        functools.partial(expert_kernel, cap),
        out_shape=jax.ShapeDtypeStruct(x.shape, jnp.bfloat16),
        grid=(blocks // group,),
        in_specs=[
            pl.BlockSpec((group, top, rows), lambda i: (i, 0, 0)),
            pl.BlockSpec((group, top, rows), lambda i: (i, 0, 0)),
            pl.BlockSpec((group, rows, width), lambda i: (i, 0, 0)),
            whole(gate.shape),
            whole(up.shape),
            whole(down.shape),
        ],
        out_specs=pl.BlockSpec((group, rows, width), lambda i: (i, 0, 0)),
        scratch_shapes=[
            pltpu.VMEM((group * cap, width), jnp.bfloat16),
            pltpu.VMEM((group * cap, width), jnp.bfloat16),
        ],
        compiler_params=pltpu.CompilerParams(vmem_limit_bytes=56 * 1024 * 1024),
        cost_estimate=pl.CostEstimate(
            flops=6 * blocks * cap * width * hidden,
            bytes_accessed=4 * blocks * rows * width + 6 * width * hidden,
            transcendentals=blocks * cap * hidden,
        ),
    )(ids, shares, x, gate, up, down)


def load_of(all_ids, hot_plan, n_rep, n_ep, routed):
    devices = n_rep * n_ep
    expert_range = jnp.arange(devices, dtype=jnp.int32)
    by_row = all_ids.reshape(n_rep, 1, -1)
    row_counts = jnp.sum(
        (by_row == expert_range.astype(jnp.float32)[None, :, None]).astype(jnp.float32), axis=2
    ).astype(jnp.int32)
    hot_flag = (expert_range // n_ep) == jnp.tile(hot_plan, n_rep)
    counts = jnp.sum(row_counts, axis=0, dtype=jnp.int32)
    copy_rows = jnp.sum(
        jnp.where(hot_flag[None, :], row_counts, 0).reshape(n_rep, n_rep, n_ep), axis=1, dtype=jnp.int32
    ).reshape(-1)
    served = jnp.where(hot_flag, jnp.zeros_like(counts), counts) + copy_rows
    return served.astype(jnp.float32) / jnp.float32(routed)


def local(tokens, expert_ids, route_weight, hot_plan, gate_proj, up_proj, down_proj):
    n_rep = lax.axis_size("rep")
    n_ep = lax.axis_size("ep")
    devices = n_rep * n_ep
    tok_rows, top = expert_ids.shape
    width = tokens.shape[1]
    routed = tok_rows * top
    hot_cap = max(16, 2 * routed // devices)
    shares = route_weight / jnp.sum(route_weight, axis=1, keepdims=True)
    told = jnp.concatenate([expert_ids.astype(jnp.float32).T, shares.T], axis=0)
    all_told = lax.all_gather(told, AXES)
    all_ids, all_shares = all_told[:, :top], all_told[:, top:]
    served_load = load_of(all_ids, hot_plan, n_rep, n_ep, routed)
    chunks = max(1, devices * tok_rows * width * 2 // (32 * 1024 * 1024))
    rows = tok_rows // chunks
    outs = []
    for i in range(chunks):
        part = slice(i * rows, (i + 1) * rows)
        x = lax.all_gather(tokens[part], AXES)
        y = run_expert(
            x, all_ids[:, :, part], all_shares[:, :, part], gate_proj[0], up_proj[0], down_proj[0], min(hot_cap, rows)
        )
        outs.append(lax.psum_scatter(y, AXES, scatter_dimension=0, tiled=False))
    out = outs[0] if chunks == 1 else jnp.concatenate(outs, axis=0)
    return (out, served_load)


def solution(mesh):
    placed = (
        P(AXES, None),
        P(AXES, None),
        P(AXES, None),
        P(),
        P(AXES, None, None),
        P(AXES, None, None),
        P(AXES, None, None),
    )
    return jax.shard_map(
        local, mesh=mesh, in_specs=placed, out_specs=(P(AXES, None), P()), check_vma=False
    )
```

time: 450 us -> 532 us (1.18)
  waiting for transfers between devices: 210 us -> 403 us
  local copies, waits for them, and re-layouts: 45.5 us -> 1.89 us
  Pallas kernels: 0 us -> 38.5 us
  matrix products: 32.3 us -> 0 us
  other arithmetic: 30.2 us -> 3.27 us
  starting transfers between devices: 24.1 us -> 0.08 us
  blocking collectives: 89.7 us -> 68.3 us
    reduce_scatter x0 -> x1, waiting for transfers between devices: none -> 354 us  [local(): outs.append(lax.psum_scatter(y, AXES, scatter_dimension=0, tiled=False))]
    psum x1 -> x0, waiting for transfers between devices: 163 us -> none  [from_root(): return lax.psum(jnp.where(mine, array, jnp.zeros_like(array)), axis)]
    psum x1 -> x0, blocking collectives: 89.7 us -> none  [local(): row_counts = lax.psum(placed, ('rep', 'ep'))]
    all_gather x0 -> x1, blocking collectives: none -> 68.3 us  [local(): all_told = lax.all_gather(told, AXES)]
    all_gather x0 -> x1, waiting for transfers between devices: none -> 47.9 us  [local(): x = lax.all_gather(tokens[part], AXES)]
    all_to_all x4 -> x0, waiting for transfers between devices: 46.3 us -> none  [the longest x1 26.8 us: local(): lax.all_to_all(copy_done, 'ep', split_axis=0, concat_axis=0, tiled=True)]
    pallas_call x0 -> x1, Pallas kernels: none -> 38.5 us  [run_expert(): pl.pallas_call(functools.partial(expert_kernel, cap), out_shape=jax.Shape...]
    dot_general x4 -> x0, matrix products: 32.3 us -> none  [the longest x2 20.5 us: expert_ffn(): jnp.dot(hidden, down_mat, preferred_element_type=jnp.float32)]
  transfers between devices with their start and end apart: 5 -> 2, of which waited for: 3 -> 2; matrix products, arithmetic and copies ran while one was open for 14% -> 1% of each run, Pallas kernels for 0% -> 0%
where the time goes in v1:
time: 532 us; the launch traced here: 529 us
  waiting for transfers between devices  403 us (76%)
  blocking collectives  68.3 us (13%)
  Pallas kernels  38.5 us (7%)
  between operations  14.1 us (3%)
    reduce_scatter x1, waiting for transfers between devices, local(): outs.append(lax.psum_scatter(y, AXES, scatter_dimension=0, tiled=False))  354 us
    all_gather x1, blocking collectives, local(): all_told = lax.all_gather(told, AXES)  68.3 us
    all_gather x1, waiting for transfers between devices, local(): x = lax.all_gather(tokens[part], AXES)  47.9 us
    pallas_call x1, Pallas kernels, run_expert(): pl.pallas_call(functools.partial(expert_kernel, cap), out_shape=jax.Shape...  38.5 us
  transfers between devices with their start and end apart: 2, of which 2 were waited for; matrix products, arithmetic and copies ran while one was open for 1% of the time, Pallas kernels for 0%

profile of v1, /device:TPU:8, one launch (start us, length us, event | category | flops | bytes accessed | tf_op | source)
XLA Modules:
  0.0 529.0 jit_solution(14325498841704221571)
XLA Ops:
  7.2 0.0 all-gather.4.cloned.1.call-start
  7.2 0.7 all-gather.4.cloned.1.call-update
  7.9 0.0 reduce-scatter.2.cloned.1.call-start
  7.9 0.7 reduce_sum.36
  8.6 0.7 convert_bitcast_fusion
  9.3 0.7 divide_bitcast_fusion
  10.0 68.3 %all-gather = f32[512,128]{1,0:T(8,128)S(1)} all-gather(f32[16,128]{1,0:T(8,128)S(1)} %pad_maximum_fusion), channel_id=2, replica_groups=mesh['rep'=4,'ep'=8] {'rep','ep'}, dimensions={0}, use_global_device_ids=true | all-gather | bytes 270336 | tf_op jit(solution)/shard_map/all_gather | solution.py:113
  78.3 0.7 fusion.3
  79.0 47.9 %all-gather.4.cloned.1.call-done = bf16[4096,2048]{1,0:T(8,128)(2,1)} async-done(((bf16[128,2048]{1,0:T(8,128)(2,1)}), bf16[4096,2048]{1,0:T(8,128)(2,1)}) %all-gather.4.cloned.1.call-update) | async-done | bytes 16777232 | tf_op jit(solution)/shard_map/all_gather | solution.py:121
  126.9 38.5 %shard_map.86 = bf16[32,128,2048]{2,1,0:T(8,128)(2,1)} custom-call(f32[32,8,128]{2,1,0:T(8,128)} %get-tuple-element.3.ids_ref, f32[32,8,128]{2,1,0:T(8,128)} %get-tuple-element.2.share_ref, bf16[32,128,2048]{2,1,0:T(8,128)(2,1)} %bitcast.11, bf16[2048,768]{1,0:T(8,128)(2,1)} %bitcast.12, bf16[2048,768]{1,0:T(8,128)(2,1)} %bitcast.13, bf16[768,2048]{1,0:T(8,128)(2,1)} %bitcast.14), custom_call_target="tpu_custom_call" | custom-call | flops 19327352832 | bytes 42991616 | tf_op jit(solution)/shard_map/pallas_call | solution.py:61
  165.4 0.0 copy-start
  165.4 0.0 copy-start.1
  165.4 0.0 reduce-scatter.2.cloned.1.call-update
  165.5 0.9 copy-done
  166.4 0.6 convert_reduce_fusion
  167.0 0.1 convert_element_type.27
  167.1 0.0 copy-done.1
  167.1 0.1 reshape.42
  167.2 0.1 tile.10
  167.3 0.5 convert_multiply_fusion
  167.8 354.3 %reduce-scatter.2.cloned.1.call-done = bf16[1,128,2048]{2,1,0:T(8,128)(2,1)} async-done(((bf16[32,128,2048]{2,1,0:T(8,128)(2,1)}), bf16[1,128,2048]{2,1,0:T(8,128)(2,1)}) %reduce-scatter.2.cloned.1.call-update) | async-done | bytes 524304 | tf_op jit(solution)/shard_map/reduce_scatter | solution.py:125
  (8 shorter events, 0.1 us)
Async XLA Ops:
  7.2 119.8 %all-gather.4.cloned.1.call-start = ((), (), s32[]{:S(2)}) async-start(), calls=%async_computation.2 | async-start | bytes 17301504 | tf_op jit(solution)/shard_map/all_gather | solution.py:121
  7.9 514.3 %reduce-scatter.2.cloned.1.call-start = ((), (), s32[]{:S(2)}) async-start(), calls=%async_computation.1 | async-start | bytes 17301504 | tf_op jit(solution)/shard_map/reduce_scatter | solution.py:125
  165.4 0.9 copy-start
  165.4 1.7 copy-start.1
Sparse Core Ops, SparseCore 0:
  11.1 115.8 all-gather.3
  165.6 356.5 reduce-scatter.1

commit v2 on v1

--- a/solution.py
+++ b/solution.py
@@ -84,6 +84,210 @@
     )(ids, shares, x, gate, up, down)
 
 
+def sum_kernel(y_ref, out_ref, held, r0, r1a, r1b, r2a, r2b, from_left, from_right, load, send, recv):
+    n_z, rows, width = y_ref.shape[2], y_ref.shape[4], y_ref.shape[5]
+    half = width // 2
+    rep, ep = lax.axis_index("rep"), lax.axis_index("ep")
+    x, core, z, y = rep // 2, rep % 2, ep // 2, ep % 2
+    ox, oy = 1 - x, 1 - y
+    to_core = (2 * x + 1 - core, ep)
+    to_x = (2 * ox + core, ep)
+    to_y = (rep, 2 * z + oy)
+    to_left = (rep, (ep + 2 * n_z - 2) % (2 * n_z))
+    to_right = (rep, (ep + 2) % (2 * n_z))
+    left, right = pl.ds(0, half), pl.ds(half, half)
+
+    barrier = pltpu.get_barrier_semaphore()
+
+    def greet(who):
+        pl.semaphore_signal(barrier, inc=1, device_id=who, device_id_type=pl.DeviceIdType.MESH)
+
+    greet(to_core)
+    greet(to_x)
+    greet(to_y)
+
+    @pl.when(z > 0)
+    def _():
+        greet(to_left)
+
+    @pl.when(z < n_z - 1)
+    def _():
+        greet(to_right)
+
+    peers = 3 + (z > 0).astype(jnp.int32) + (z < n_z - 1).astype(jnp.int32)
+    pl.semaphore_wait(barrier, peers)
+
+    def remote(src, dst, kind, k, who):
+        return pltpu.make_async_remote_copy(
+            src_ref=src,
+            dst_ref=dst,
+            send_sem=send.at[kind, k],
+            recv_sem=recv.at[kind, k],
+            device_id=who,
+            device_id_type=pl.DeviceIdType.MESH,
+        )
+
+    def copy_core(k):
+        return remote(y_ref.at[:, 1 - core, k], r0.at[k], 0, k, to_core)
+
+    def copy_own(k):
+        return pltpu.make_async_copy(y_ref.at[:, core, k], held.at[k], load.at[k])
+
+    def copies_1(k):
+        return (
+            remote(held.at[k, ox, :, :, left], r1a.at[k], 1, k, to_x),
+            remote(held.at[k, :, oy, :, right], r1b.at[k], 2, k, to_y),
+        )
+
+    def copies_2(k):
+        return (
+            remote(held.at[k, x, oy, :, left], r2a.at[k], 3, k, to_y),
+            remote(held.at[k, ox, y, :, right], r2b.at[k], 4, k, to_x),
+        )
+
+    def copy_right(k):
+        return remote(held.at[k, x, y], from_left.at[k], 5, k, to_right)
+
+    def copy_left(k):
+        return remote(held.at[k, x, y], from_right.at[k], 6, k, to_left)
+
+    step = 16
+
+    def over_rows(body):
+        @pl.loop(0, rows // step)
+        def _(i):
+            body(pl.ds(pl.multiple_of(i * step, step), step))
+
+    def take_core(k):
+        copy_own(k).wait()
+        copy_core(k).wait_recv()
+
+        def body(at):
+            for i in range(2):
+                for j in range(2):
+                    held[k, i, j, at, :] = held[k, i, j, at, :] + r0[k, i, j, at, :]
+
+        over_rows(body)
+        for c in copies_1(k):
+            c.start()
+
+    def take_1(k):
+        for c in copies_1(k):
+            c.wait_recv()
+
+        def body(at):
+            for i in range(2):
+                held[k, x, i, at, left] = held[k, x, i, at, left] + r1a[k, i, at, :]
+                held[k, i, y, at, right] = held[k, i, y, at, right] + r1b[k, i, at, :]
+
+        over_rows(body)
+        for c in copies_2(k):
+            c.start()
+
+    def take_2(k):
+        for c in copies_2(k):
+            c.wait_recv()
+
+        def body(at):
+            held[k, x, y, at, left] = held[k, x, y, at, left] + r2a[k, at, :]
+            held[k, x, y, at, right] = held[k, x, y, at, right] + r2b[k, at, :]
+
+        over_rows(body)
+
+    def take_z(k):
+        if k > 0:
+
+            @pl.when((z > 0) & (z <= k))
+            def _():
+                copy_right(k).wait_recv()
+
+                def body(at):
+                    held[k, x, y, at, :] = held[k, x, y, at, :] + from_left[k, at, :]
+
+                over_rows(body)
+
+            @pl.when(z < k)
+            def _():
+                copy_right(k).start()
+
+        if k < n_z - 1:
+
+            @pl.when((z < n_z - 1) & (z >= k))
+            def _():
+                copy_left(k).wait_recv()
+
+                def body(at):
+                    held[k, x, y, at, :] = held[k, x, y, at, :] + from_right[k, at, :]
+
+                over_rows(body)
+
+            @pl.when(z > k)
+            def _():
+                copy_left(k).start()
+
+        @pl.when(z == k)
+        def _():
+            def body(at):
+                out_ref[at, :] = held[k, x, y, at, :]
+
+            over_rows(body)
+
+    order = []
+    for k in range((n_z + 1) // 2):
+        order += [n_z - 1 - k, k] if n_z - 1 - k != k else [k]
+    for k in order:
+        copy_core(k).start()
+        copy_own(k).start()
+    for t in range(n_z + 3):
+        for late, stage in enumerate((take_core, take_1, take_2, take_z)):
+            if 0 <= t - late < n_z:
+                stage(order[t - late])
+    for k in order:
+        copy_core(k).wait_send()
+        for c in copies_1(k) + copies_2(k):
+            c.wait_send()
+        if k > 0:
+
+            @pl.when(z < k)
+            def _():
+                copy_right(k).wait_send()
+
+        if k < n_z - 1:
+
+            @pl.when(z > k)
+            def _():
+                copy_left(k).wait_send()
+
+
+def sum_blocks(y, n_rep, n_ep):
+    rows, width = y.shape[1:]
+    n_z, half = n_ep // 2, width // 2
+    assert n_rep == 4 and n_ep % 2 == 0
+    vmem = lambda *shape: pltpu.VMEM(shape, jnp.bfloat16)
+    return pl.pallas_call(
+        sum_kernel,
+        out_shape=jax.ShapeDtypeStruct((rows, width), jnp.bfloat16),
+        in_specs=[pl.BlockSpec(memory_space=pl.ANY)],
+        out_specs=pl.BlockSpec(memory_space=pltpu.VMEM),
+        scratch_shapes=[
+            vmem(n_z, 2, 2, rows, width),
+            vmem(n_z, 2, 2, rows, width),
+            vmem(n_z, 2, rows, half),
+            vmem(n_z, 2, rows, half),
+            vmem(n_z, rows, half),
+            vmem(n_z, rows, half),
+            vmem(n_z, rows, width),
+            vmem(n_z, rows, width),
+            pltpu.SemaphoreType.DMA((n_z,)),
+            pltpu.SemaphoreType.DMA((7, n_z)),
+            pltpu.SemaphoreType.DMA((7, n_z)),
+        ],
+        compiler_params=pltpu.CompilerParams(
+            collective_id=0, has_side_effects=True, vmem_limit_bytes=56 * 1024 * 1024
+        ),
+    )(y.reshape(2, 2, n_z, 2, rows, width))
+
+
 def load_of(all_ids, hot_plan, n_rep, n_ep, routed):
     devices = n_rep * n_ep
     expert_range = jnp.arange(devices, dtype=jnp.int32)
@@ -113,7 +317,7 @@
     all_told = lax.all_gather(told, AXES)
     all_ids, all_shares = all_told[:, :top], all_told[:, top:]
     served_load = load_of(all_ids, hot_plan, n_rep, n_ep, routed)
-    chunks = max(1, devices * tok_rows * width * 2 // (32 * 1024 * 1024))
+    chunks = max(1, devices * tok_rows * width * 2 // (16 * 1024 * 1024))
     rows = tok_rows // chunks
     outs = []
     for i in range(chunks):
@@ -122,7 +326,7 @@
         y = run_expert(
             x, all_ids[:, :, part], all_shares[:, :, part], gate_proj[0], up_proj[0], down_proj[0], min(hot_cap, rows)
         )
-        outs.append(lax.psum_scatter(y, AXES, scatter_dimension=0, tiled=False))
+        outs.append(sum_blocks(y, n_rep, n_ep))
     out = outs[0] if chunks == 1 else jnp.concatenate(outs, axis=0)
     return (out, served_load)
 

time: 532 us -> 326 us (0.61)
  waiting for transfers between devices: 403 us -> 45.8 us
  Pallas kernels: 38.5 us -> 190 us
    reduce_scatter x1 -> x0, waiting for transfers between devices: 354 us -> none  [local(): outs.append(lax.psum_scatter(y, AXES, scatter_dimension=0, tiled=False))]
    pallas_call x0 -> x1, Pallas kernels: none -> 151 us  [sum_blocks(): pl.pallas_call(sum_kernel, out_shape=jax.ShapeDtypeStruct((rows, width),...]
  transfers between devices with their start and end apart: 2 -> 1, of which waited for: 2 -> 1; matrix products, arithmetic and copies ran while one was open for 1% -> 2% of each run, Pallas kernels for 0% -> 0%
where the time goes in v2:
time: 326 us; the launch traced here: 325 us
  Pallas kernels  190 us (58%)
  blocking collectives  68.3 us (21%)
  waiting for transfers between devices  45.8 us (14%)
  between operations  14.1 us (4%)
  other arithmetic  3.93 us (1%)
  local copies, waits for them, and re-layouts  3.52 us (1%)
    pallas_call x1, Pallas kernels, sum_blocks(): pl.pallas_call(sum_kernel, out_shape=jax.ShapeDtypeStruct((rows, width),...  151 us
    all_gather x1, blocking collectives, local(): all_told = lax.all_gather(told, AXES)  68.3 us
    all_gather x1, waiting for transfers between devices, local(): x = lax.all_gather(tokens[part], AXES)  45.1 us
    pallas_call x1, Pallas kernels, run_expert(): pl.pallas_call(functools.partial(expert_kernel, cap), out_shape=jax.Shape...  38.5 us
  transfers between devices with their start and end apart: 1, of which 1 were waited for; matrix products, arithmetic and copies ran while one was open for 2% of the time, Pallas kernels for 0%

profile of v2, /device:TPU:8, one launch (start us, length us, event | category | flops | bytes accessed | tf_op | source)
XLA Modules:
  0.0 325.4 jit_solution(12609249482810655934)
XLA Ops:
  7.2 0.0 all-gather.4.cloned.1.call-start
  7.2 0.7 all-gather.4.cloned.1.call-update
  7.9 0.7 reduce_sum.36
  8.6 0.7 convert_bitcast_fusion
  9.3 0.7 divide_bitcast_fusion
  10.0 68.3 %all-gather = f32[512,128]{1,0:T(8,128)S(1)} all-gather(f32[16,128]{1,0:T(8,128)S(1)} %pad_maximum_fusion), channel_id=2, replica_groups=mesh['rep'=4,'ep'=8] {'rep','ep'}, dimensions={0}, use_global_device_ids=true | all-gather | bytes 270336 | tf_op jit(solution)/shard_map/all_gather | solution.py:317
  78.3 0.7 fusion.3
  78.9 0.0 copy-start
  79.0 0.6 convert_reduce_fusion
  79.6 0.1 convert_element_type.27
  79.7 0.7 fusion
  80.4 0.1 reshape.46
  80.5 0.7 tile.4
  81.1 0.1 tile.10
  81.2 0.5 convert_multiply_fusion
  81.8 45.1 %all-gather.4.cloned.1.call-done = bf16[4096,2048]{1,0:T(8,128)(2,1)} async-done(((bf16[128,2048]{1,0:T(8,128)(2,1)}), bf16[4096,2048]{1,0:T(8,128)(2,1)}) %all-gather.4.cloned.1.call-update) | async-done | bytes 16777232 | tf_op jit(solution)/shard_map/all_gather | solution.py:325
  126.9 0.0 copy-done
  126.9 38.5 %shard_map.86 = bf16[32,128,2048]{2,1,0:T(8,128)(2,1)} custom-call(f32[32,8,128]{2,1,0:T(8,128)} %copy-done, f32[32,8,128]{2,1,0:T(8,128)} %get-tuple-element.2.share_ref, bf16[32,128,2048]{2,1,0:T(8,128)(2,1)} %bitcast.12, bf16[2048,768]{1,0:T(8,128)(2,1)} %bitcast.13, bf16[2048,768]{1,0:T(8,128)(2,1)} %bitcast.14, bf16[768,2048]{1,0:T(8,128)(2,1)} %bitcast.15), custom_call_target="tpu_custom_call" | custom-call | flops 19327352832 | bytes 42991616 | tf_op jit(solution)/shard_map/pallas_call | solution.py:61
  165.4 151.3 %shard_map.87 = bf16[128,2048]{1,0:T(8,128)(2,1)} custom-call(bf16[2,2,4,2,128,2048]{5,4,3,2,1,0:T(8,128)(2,1)} %bitcast.10), custom_call_target="tpu_custom_call" | custom-call | tf_op jit(solution)/shard_map/pallas_call | solution.py:267
  316.7 1.9 copy.10
  (6 shorter events, 0.1 us)
Async XLA Ops:
  7.2 119.7 %all-gather.4.cloned.1.call-start = ((), (), s32[]{:S(2)}) async-start(), calls=%async_computation | async-start | bytes 17301504 | tf_op jit(solution)/shard_map/all_gather | solution.py:325
  78.9 47.9 %copy-start = (f32[32,8,128]{2,1,0:T(8,128)}, f32[32,8,128]{2,1,0:T(8,128)S(1)}, u32[]{:S(2)}) copy-start(f32[32,8,128]{2,1,0:T(8,128)S(1)} %get-tuple-element.3.ids_ref) | copy-start | bytes 393220
Sparse Core Ops, SparseCore 0:
  11.1 115.7 all-gather.3

commit v3 on v2

--- a/solution.py
+++ b/solution.py
@@ -17,39 +17,51 @@
         jnp.int32, (rows, rows), 1
     )
     earlier = earlier.astype(jnp.bfloat16)
-    slots = lax.broadcasted_iota(jnp.int32, (cap, rows), 0).astype(jnp.float32)
+    pair = 2 if blocks % 2 == 0 else 1
+    places = lax.broadcasted_iota(jnp.int32, (pair * cap, pair * rows), 0).astype(jnp.float32)
     picks = []
     scales = []
-    for b in range(blocks):
-        match = ids_ref[b] == me
-        weight = jnp.sum(jnp.where(match, share_ref[b], 0.0), axis=0, keepdims=True)
-        named = jnp.max(match.astype(jnp.float32), axis=0, keepdims=True)
-        before = jnp.dot(
-            jnp.broadcast_to(named, (8, rows)).astype(jnp.bfloat16),
-            earlier,
+    for p in range(blocks // pair):
+        targets = []
+        weights = []
+        for q in range(pair):
+            match = ids_ref[p * pair + q] == me
+            weights.append(jnp.sum(jnp.where(match, share_ref[p * pair + q], 0.0), axis=0, keepdims=True))
+            named = jnp.max(match.astype(jnp.float32), axis=0, keepdims=True)
+            before = jnp.dot(
+                jnp.broadcast_to(named, (8, rows)).astype(jnp.bfloat16),
+                earlier,
+                preferred_element_type=jnp.float32,
+            )[0:1]
+            targets.append(jnp.where(named > 0.0, before + q * cap, -1.0))
+        pick = jnp.where(places == jnp.concatenate(targets, axis=1), 1.0, 0.0)
+        picks.append(pick.astype(jnp.bfloat16))
+        scales.append(jnp.sum(pick * jnp.concatenate(weights, axis=1), axis=1, keepdims=True))
+        sel[p * pair * cap : (p + 1) * pair * cap, :] = jnp.dot(
+            picks[p],
+            x_ref[p * pair : (p + 1) * pair].reshape(pair * rows, x_ref.shape[2]),
             preferred_element_type=jnp.float32,
-        )[0:1]
-        hit = (slots == before) & (named > 0.0)
-        pick = jnp.where(hit, 1.0, 0.0)
-        picks.append(pick.astype(jnp.bfloat16))
-        scales.append(jnp.sum(pick * weight, axis=1, keepdims=True))
-        sel[b * cap : (b + 1) * cap, :] = jnp.dot(
-            picks[b], x_ref[b], preferred_element_type=jnp.float32
         ).astype(jnp.bfloat16)
     gate_in = jnp.dot(sel[...], gate_ref[...], preferred_element_type=jnp.float32)
     up_in = jnp.dot(sel[...], up_ref[...], preferred_element_type=jnp.float32)
     hidden = (gate_in / (1.0 + jnp.exp(-gate_in)) * up_in).astype(jnp.bfloat16)
-    done = jnp.dot(hidden, down_ref[...], preferred_element_type=jnp.float32)
-    for b in range(blocks):
-        part = slice(b * cap, (b + 1) * cap)
-        res[part, :] = (done[part] * scales[b]).astype(jnp.bfloat16)
-    for b in range(blocks):
-        out_ref[b] = lax.dot_general(
-            picks[b],
-            res[b * cap : (b + 1) * cap, :],
-            (((0,), (0,)), ((), ())),
-            preferred_element_type=jnp.float32,
-        ).astype(jnp.bfloat16)
+    scale = jnp.concatenate(scales, axis=0)
+    width = x_ref.shape[2]
+    part = width // 4 if width % 512 == 0 else width
+    for at in range(0, width, part):
+        done = jnp.dot(hidden, down_ref[:, at : at + part], preferred_element_type=jnp.float32)
+        res[:, at : at + part] = (done * scale).astype(jnp.bfloat16)
+        for p in range(blocks // pair):
+            out_ref[p * pair : (p + 1) * pair, :, at : at + part] = (
+                lax.dot_general(
+                    picks[p],
+                    res[p * pair * cap : (p + 1) * pair * cap, at : at + part],
+                    (((0,), (0,)), ((), ())),
+                    preferred_element_type=jnp.float32,
+                )
+                .astype(jnp.bfloat16)
+                .reshape(pair, rows, part)
+            )
 
 
 def run_expert(x, ids, shares, gate, up, down, cap):

time: 326 us -> 324 us (level)
  no operation moved by 1% of the time
where the time goes in v3:
time: 324 us
  Pallas kernels  188 us (58%)
  blocking collectives  68.3 us (21%)
  waiting for transfers between devices  45.8 us (14%)
  between operations  14.1 us (4%)
  other arithmetic  3.93 us (1%)
  local copies, waits for them, and re-layouts  3.52 us (1%)
    pallas_call x1, Pallas kernels, sum_blocks(): pl.pallas_call(sum_kernel, out_shape=jax.ShapeDtypeStruct((rows, width),...  151 us
    all_gather x1, blocking collectives, local(): all_told = lax.all_gather(told, AXES)  68.3 us
    all_gather x1, waiting for transfers between devices, local(): x = lax.all_gather(tokens[part], AXES)  45.1 us
    pallas_call x1, Pallas kernels, run_expert(): pl.pallas_call(functools.partial(expert_kernel, cap), out_shape=jax.Shape...  36.8 us
  transfers between devices with their start and end apart: 1, of which 1 were waited for; matrix products, arithmetic and copies ran while one was open for 2% of the time, Pallas kernels for 0%

profile of v3, /device:TPU:8, one launch (start us, length us, event | category | flops | bytes accessed | tf_op | source)
XLA Modules:
  0.0 323.6 jit_solution(11904665784120453682)
XLA Ops:
  7.2 0.0 all-gather.4.cloned.1.call-start
  7.2 0.7 all-gather.4.cloned.1.call-update
  7.9 0.7 reduce_sum.36
  8.6 0.7 convert_bitcast_fusion
  9.3 0.7 divide_bitcast_fusion
  10.0 68.3 %all-gather = f32[512,128]{1,0:T(8,128)S(1)} all-gather(f32[16,128]{1,0:T(8,128)S(1)} %pad_maximum_fusion), channel_id=2, replica_groups=mesh['rep'=4,'ep'=8] {'rep','ep'}, dimensions={0}, use_global_device_ids=true | all-gather | bytes 270336 | tf_op jit(solution)/shard_map/all_gather | solution.py:329
  78.3 0.7 fusion.3
  78.9 0.0 copy-start
  79.0 0.6 convert_reduce_fusion
  79.6 0.1 convert_element_type.27
  79.7 0.7 fusion
  80.4 0.1 reshape.46
  80.5 0.7 tile.4
  81.1 0.1 tile.10
  81.2 0.5 convert_multiply_fusion
  81.8 45.1 %all-gather.4.cloned.1.call-done = bf16[4096,2048]{1,0:T(8,128)(2,1)} async-done(((bf16[128,2048]{1,0:T(8,128)(2,1)}), bf16[4096,2048]{1,0:T(8,128)(2,1)}) %all-gather.4.cloned.1.call-update) | async-done | bytes 16777232 | tf_op jit(solution)/shard_map/all_gather | solution.py:337
  126.9 0.0 copy-done
  126.9 36.8 %shard_map.86 = bf16[32,128,2048]{2,1,0:T(8,128)(2,1)} custom-call(f32[32,8,128]{2,1,0:T(8,128)} %copy-done, f32[32,8,128]{2,1,0:T(8,128)} %get-tuple-element.2.share_ref, bf16[32,128,2048]{2,1,0:T(8,128)(2,1)} %bitcast.12, bf16[2048,768]{1,0:T(8,128)(2,1)} %bitcast.13, bf16[2048,768]{1,0:T(8,128)(2,1)} %bitcast.14, bf16[768,2048]{1,0:T(8,128)(2,1)} %bitcast.15), custom_call_target="tpu_custom_call" | custom-call | flops 19327352832 | bytes 42991616 | tf_op jit(solution)/shard_map/pallas_call | solution.py:73
  163.7 151.2 %shard_map.87 = bf16[128,2048]{1,0:T(8,128)(2,1)} custom-call(bf16[2,2,4,2,128,2048]{5,4,3,2,1,0:T(8,128)(2,1)} %bitcast.10), custom_call_target="tpu_custom_call" | custom-call | tf_op jit(solution)/shard_map/pallas_call | solution.py:279
  314.9 1.9 copy.10
  (6 shorter events, 0.1 us)
Async XLA Ops:
  7.2 119.7 %all-gather.4.cloned.1.call-start = ((), (), s32[]{:S(2)}) async-start(), calls=%async_computation | async-start | bytes 17301504 | tf_op jit(solution)/shard_map/all_gather | solution.py:337
  78.9 47.9 %copy-start = (f32[32,8,128]{2,1,0:T(8,128)}, f32[32,8,128]{2,1,0:T(8,128)S(1)}, u32[]{:S(2)}) copy-start(f32[32,8,128]{2,1,0:T(8,128)S(1)} %get-tuple-element.3.ids_ref) | copy-start | bytes 393220
Sparse Core Ops, SparseCore 0:
  11.1 115.7 all-gather.3
